TPU v7x, 32 devices: a whole 2x2x4 slice. The times are simulated.
32 devices in a mesh: dp: 8 (over z, y), rep: 4 (over x, core).
Axes of the slice: x: 2, y: 2, z: 4, core: 2. Of those that a mesh axis runs over, the one named last changes fastest.
Arguments:
- tokens: bfloat16 [1024, 2048], P('dp'), may hold values from -6 to 6
- cotangent: bfloat16 [1024, 2048], P('dp'), may hold values from -6 to 6
- probe_seed: int32 [1024], P('dp'), may hold values from 0 to 1073741823
- w_in: bfloat16 [2048, 8192], P('dp', 'rep'), may hold values from -0.125 to 0.125
- bias: float32 [8192], P('rep'), may hold values from -1.5 to 1.5
- w_out: bfloat16 [8192, 2048], P(('rep', 'dp')), may hold values from -0.0625 to 0.0625
- left_in: bfloat16 [2048], replicated, may hold values from -6 to 6
- left_out: bfloat16 [8192], P('rep'), may hold values from -6 to 6
Outputs:
- output: bfloat16 [1024, 2048], P('dp')
- logdet: float32 [1024], P('dp')
- grad_tokens: float32 [1024, 2048], P('dp')
- grad_in: float32 [2048, 8192], P('dp', 'rep')
- grad_out: float32 [8192, 2048], P(('rep', 'dp'))
All inputs are finite; a program needn't handle non-finite values.
Results may differ from a plain program's by a relative error of at most 0.012.
Values may be sent and summed in bfloat16 or wider, within the bound.
No kernel may reach another device: no remote copies, remote signals or barrier semaphores. Data moves between devices by JAX's collectives and lax.ppermute only.
A program may use at most 128 MiB of HBM per device.

v0:
```python
import jax
import jax.numpy as jnp
from jax import lax
from jax.sharding import PartitionSpec as P


def probe_signs(seeds, width):
    columns = jnp.arange(width, dtype=jnp.int32)
    mixed = seeds[:, None] * 747796405 + columns[None, :] * 1640531527
    mixed = mixed ^ lax.shift_right_logical(mixed, jnp.full_like(mixed, 16))
    mixed = mixed * 668265261
    mixed = mixed ^ lax.shift_right_logical(mixed, jnp.full_like(mixed, 15))
    lowbit = jnp.bitwise_and(lax.shift_right_logical(mixed, jnp.full_like(mixed, 7)), 1)
    return (1 - 2 * lowbit).astype(jnp.float32).astype(jnp.bfloat16)


def contract_rows(left, right):
    return lax.dot_general(
        left, right, (((0,), (0,)), ((), ())), preferred_element_type=jnp.float32
    )


def contract_cols(left, right):
    return lax.dot_general(
        left, right, (((1,), (1,)), ((), ())), preferred_element_type=jnp.float32
    )


def front_layer(raw, bias, scale_in, count):
    z_pre = scale_in * raw[:count] + bias
    e_one = scale_in * raw[count:]
    tanh_z = jnp.tanh(z_pre)
    deriv = 1.0 - tanh_z * tanh_z
    second = -2.0 * tanh_z * deriv
    act = tanh_z.astype(jnp.bfloat16)
    r_one = (e_one * deriv).astype(jnp.bfloat16)
    return (e_one, act, deriv, second, r_one)


def on_device(tokens, cotangent, probe_seed, w_in, bias, w_out, left_in, left_out):
    coef = 0.9
    count = tokens.shape[0]
    width = tokens.shape[1]
    rows_in = w_in.shape[0]
    rows_out = w_out.shape[0]
    probe = probe_signs(probe_seed, width)
    stacked_in = jnp.concatenate([tokens, probe], 0)
    left_one = left_in.astype(jnp.float32)
    left_two = left_out.astype(jnp.float32)
    un_one = jnp.sum(left_one * left_one)
    full_in = lax.all_gather(w_in, "dp", axis=0, tiled=True)
    full_out = lax.all_gather(w_out, "dp", axis=0, tiled=True)
    raw = jnp.dot(stacked_in, full_in, preferred_element_type=jnp.float32)
    p_vec = jnp.dot(left_in, full_in, preferred_element_type=jnp.float32)
    q_part = jnp.dot(left_out, full_out, preferred_element_type=jnp.float32)
    p_norm, q_vec, un_two = lax.psum(
        (jnp.sum(p_vec * p_vec), q_part, jnp.sum(left_two * left_two)), "rep"
    )
    scale_in = coef * jnp.sqrt(un_one / p_norm)
    e_one, act, deriv, second, r_one = front_layer(raw, bias, scale_in, count)
    stacked_hidden = jnp.concatenate([act, r_one], 0)
    out_raw = jnp.dot(stacked_hidden, full_out, preferred_element_type=jnp.float32)
    q_norm = jnp.sum(q_vec * q_vec)
    scale_out = coef * jnp.sqrt(un_two / q_norm)
    branch_part = scale_out * out_raw[:count]
    j_one_part = scale_out * out_raw[count:]
    branch_all, j_one_all = lax.psum((branch_part, j_one_part), "rep")
    output = (tokens.astype(jnp.float32) + branch_all).astype(jnp.bfloat16)
    j_one = j_one_all.astype(jnp.bfloat16)
    e_two = scale_in * jnp.dot(j_one, full_in, preferred_element_type=jnp.float32)
    r_two = (e_two * deriv).astype(jnp.bfloat16)
    j_two_part = scale_out * jnp.dot(r_two, full_out, preferred_element_type=jnp.float32)
    j_two = lax.psum(j_two_part.astype(jnp.bfloat16), "rep")
    e_three = scale_in * jnp.dot(j_two, full_in, preferred_element_type=jnp.float32)
    backs = scale_out * contract_cols(jnp.concatenate([probe, cotangent], 0), full_out)
    bvec = backs[:count]
    cback = backs[count:]
    hd_vec = deriv * bvec
    a_vec = e_one - e_two + e_three
    g_round = (a_vec * deriv).astype(jnp.bfloat16)
    left_two_grad = jnp.concatenate([act, g_round], 0)
    right_two_grad = jnp.concatenate([cotangent, -probe], 0)
    terms = jnp.stack(
        [
            jnp.sum(e_one * hd_vec, axis=1),
            jnp.sum(e_two * hd_vec, axis=1),
            jnp.sum(e_three * hd_vec, axis=1),
        ],
        1,
    )
    dz_vec = cback * deriv - a_vec * bvec * second
    dz_round = dz_vec.astype(jnp.bfloat16)
    dx_part = scale_in * contract_cols(dz_round, full_in)
    dx_all, terms_all = (
        lax.psum(dx_part.astype(jnp.bfloat16), "rep").astype(jnp.float32),
        lax.psum(terms.astype(jnp.bfloat16), "rep").astype(jnp.float32),
    )
    grad_tokens = cotangent.astype(jnp.float32) + dx_all
    logdet = terms_all[:, 0] - terms_all[:, 1] / 2.0 + terms_all[:, 2] / 3.0
    w_vec = (
        probe.astype(jnp.float32) - j_one.astype(jnp.float32) + j_two.astype(jnp.float32)
    ).astype(jnp.bfloat16)
    h_round = hd_vec.astype(jnp.bfloat16)
    left_grad = jnp.concatenate([tokens, w_vec], 0)
    right_grad = jnp.concatenate([dz_round, -h_round], 0)
    grad_one = lax.psum_scatter(
        contract_rows(left_grad, right_grad), "dp", scatter_dimension=0, tiled=True
    )
    grad_two = lax.psum_scatter(
        contract_rows(left_two_grad, right_two_grad), "dp", scatter_dimension=0, tiled=True
    )
    inner_one, inner_two = lax.psum(
        (
            jnp.sum(grad_one * w_in.astype(jnp.float32)),
            jnp.sum(grad_two * w_out.astype(jnp.float32)),
        ),
        ("dp", "rep"),
    )
    dp_index = lax.axis_index("dp")
    slice_one = lax.dynamic_slice_in_dim(left_one, dp_index * rows_in, rows_in, 0)
    slice_two = lax.dynamic_slice_in_dim(left_two, dp_index * rows_out, rows_out, 0)
    grad_in = scale_in * (grad_one - inner_one * slice_one[:, None] * p_vec[None, :] / p_norm)
    grad_out = scale_out * (grad_two - inner_two * slice_two[:, None] * q_vec[None, :] / q_norm)
    return (output, logdet, grad_tokens, grad_in, grad_out)


def solution(mesh):
    placed = (
        P("dp", None),
        P("dp", None),
        P("dp"),
        P("dp", "rep"),
        P("rep"),
        P(("rep", "dp"), None),
        P(),
        P("rep"),
    )
    return jax.shard_map(
        on_device,
        mesh=mesh,
        in_specs=placed,
        out_specs=(P("dp", None), P("dp"), P("dp", None), P("dp", "rep"), P(("rep", "dp"), None)),
        check_vma=False,
    )
```

profile of v0, /device:TPU:0, one launch (start us, length us, event | category | flops | bytes accessed | tf_op | source)
XLA Modules:
  0.0 1057.2 jit_solution(5849140991647013350)
XLA Ops:
  8.0 0.7 all-gather.3.cloned.1.call-update
  10.5 127.3 %all-gather.5.cloned.1.call-done = bf16[2048,2048]{1,0:T(8,128)(2,1)} async-done(((bf16[256,2048]{1,0:T(8,128)(2,1)}), bf16[2048,2048]{1,0:T(8,128)(2,1)}) %all-gather.5.cloned.1.call-update) | async-done | bytes 8388624 | tf_op jit(solution)/shard_map/all_gather | solution.py:51
  137.8 4.6 fusion.44
  143.0 120.1 %all-gather.3.cloned.1.call-done = bf16[2048,2048]{1,0:T(8,128)(2,1)} async-done(((bf16[256,2048]{1,0:T(8,128)(2,1)}), bf16[2048,2048]{1,0:T(8,128)(2,1)}) %all-gather.3.cloned.1.call-update) | async-done | bytes 8388624 | tf_op jit(solution)/shard_map/all_gather | solution.py:52
  263.1 4.6 fusion.43
  267.7 7.1 all-reduce.1
  278.1 5.9 fusion.4
  284.3 2.4 fusion.2
  286.8 1.1 slice_multiply_fusion.1
  287.9 26.0 %all-reduce.12 = bf16[128,2048]{1,0:T(8,128)(2,1)} all-reduce(f32[128,2048]{1,0:T(8,128)S(1)} %get-tuple-element.22), channel_id=1, replica_groups=mesh['dp'=8,'rep'=4] {'rep'}, use_global_device_ids=true, to_apply=%region_9.0 | all-reduce | flops 262144 | bytes 1572864 | tf_op jit(solution)/shard_map/psum | solution.py:67
  313.9 4.8 convolution_multiply_fusion.4
  318.8 5.5 fusion
  324.5 6.2 convolution_multiply_fusion
  330.7 1.3 copy-done.3
  332.0 1.4 convert_negate_fusion
  333.5 21.9 %all-reduce.9.cloned.1.call-done = bf16[128,2048]{1,0:T(8,128)(2,1)} async-done(((bf16[128,2048]{1,0:T(8,128)(2,1)}), bf16[128,2048]{1,0:T(8,128)(2,1)}) %all-reduce.9.cloned.1.call-update) | async-done | bytes 524304 | tf_op jit(solution)/shard_map/psum | solution.py:73
  355.3 6.6 multiply_convert_fusion
  363.8 8.1 fusion.5
  373.3 8.1 fusion.3
  381.5 6.3 psum.76
  388.3 7.1 fusion.1
  395.5 2.2 add_convert_fusion.1
  397.7 283.1 %reduce-scatter.3.cloned.1.call-done = f32[256,2048]{1,0:T(8,128)} async-done(((f32[2048,2048]{1,0:T(8,128)}), f32[256,2048]{1,0:T(8,128)}) %reduce-scatter.3.cloned.1.call-update) | async-done | bytes 2097168 | tf_op jit(solution)/shard_map/reduce_scatter | solution.py:106
  680.8 2.7 multiply_reduce_fusion.1
  683.5 282.7 %reduce-scatter.5.cloned.1.call-done = f32[256,2048]{1,0:T(8,128)} async-done(((f32[2048,2048]{1,0:T(8,128)}), f32[256,2048]{1,0:T(8,128)}) %reduce-scatter.5.cloned.1.call-update) | async-done | bytes 2097168 | tf_op jit(solution)/shard_map/reduce_scatter | solution.py:109
  966.2 2.8 multiply_reduce_fusion
  969.0 32.5 %all-reduce.11.cloned.1.call-done = bf16[128,2048]{1,0:T(8,128)(2,1)} async-done(((bf16[128,2048]{1,0:T(8,128)(2,1)}), bf16[128,2048]{1,0:T(8,128)(2,1)}) %all-reduce.11.cloned.1.call-update) | async-done | bytes 524304 | tf_op jit(solution)/shard_map/psum | solution.py:95
  1001.5 2.3 convert_add_fusion
  1003.8 39.6 %all-reduce = (f32[]{:T(128)}, f32[]{:T(128)}) all-reduce(f32[]{:T(128)} %multiply_reduce_fusion.1, f32[]{:T(128)} %multiply_reduce_fusion), channel_id=1, replica_groups=mesh['dp'=8,'rep'=4] {'dp','rep'}, use_global_device_ids=true, to_apply=%region_17.0 | all-reduce | flops 2 | bytes 16 | tf_op jit(solution)/shard_map/psum | solution.py:112
  1043.4 0.7 dynamic-slice_multiply_fusion
  1044.1 0.7 dynamic-slice_multiply_fusion.1
  1044.8 5.5 subtract_multiply_fusion
  (71 shorter events, 8.1 us)
Async XLA Ops:
  7.2 1.6 copy-start.18
  7.2 1.6 copy-start.17
  7.2 2.8 copy-start.19
  7.2 130.6 %all-gather.5.cloned.1.call-start = ((), (), s32[]{:S(2)}) async-start(), calls=%async_computation.3 | async-start | bytes 9437184 | tf_op jit(solution)/shard_map/all_gather | solution.py:51
  7.9 255.2 %all-gather.3.cloned.1.call-start = ((), (), s32[]{:S(2)}) async-start(), calls=%async_computation.2 | async-start | bytes 9437184 | tf_op jit(solution)/shard_map/all_gather | solution.py:52
  8.7 346.7 %all-reduce.9.cloned.1.call-start = ((), (), s32[]{:S(2)}) async-start(), calls=%async_computation.5 | async-start | bytes 1048576 | tf_op jit(solution)/shard_map/psum | solution.py:73
  10.5 267.6 %copy-start.15 = (bf16[128,2048]{1,0:T(8,128)(2,1)}, bf16[128,2048]{1,0:T(8,128)(2,1)S(1)}, u32[]{:S(2)}) copy-start(bf16[128,2048]{1,0:T(8,128)(2,1)S(1)} %fusion.12) | copy-start | bytes 1572868
  143.0 135.1 %copy-start.8 = (bf16[128,2048]{1,0:T(8,128)(2,1)S(1)}, bf16[128,2048]{1,0:T(8,128)(2,1)}, u32[]{:S(2)}) copy-start(bf16[128,2048]{1,0:T(8,128)(2,1)} %param.8) | copy-start | bytes 1572868
  278.1 5.9 copy-start.16
  278.1 6.2 copy-start
  284.3 2.4 copy-start.11
  324.2 71.3 %all-reduce.7.cloned.1.call-start = ((), (), s32[]{:S(2)}) async-start(), calls=%async_computation.4 | async-start | bytes 2097152 | tf_op jit(solution)/shard_map/psum | solution.py:67
  330.7 1.3 copy-start.3
  333.4 347.4 %reduce-scatter.3.cloned.1.call-start = ((), (), s32[]{:S(2)}) async-start(), calls=%async_computation.7 | async-start | bytes 18874368 | tf_op jit(solution)/shard_map/reduce_scatter | solution.py:106
  355.3 6.6 copy-start.4
  362.0 1.0 copy-start.2
  362.0 1.2 copy-start.7
  362.0 1.8 copy-start.9
  362.0 1.8 copy-start.13
  371.9 1.0 copy-start.10
  371.9 1.2 copy-start.12
  371.9 1.4 copy-start.14
  371.9 594.3 %reduce-scatter.5.cloned.1.call-start = ((), (), s32[]{:S(2)}) async-start(), calls=%async_computation.8 | async-start | bytes 18874368 | tf_op jit(solution)/shard_map/reduce_scatter | solution.py:109
  381.4 620.1 %all-reduce.11.cloned.1.call-start = ((), (), s32[]{:S(2)}) async-start(), calls=%async_computation.6 | async-start | bytes 1048576 | tf_op jit(solution)/shard_map/psum | solution.py:95
  395.5 285.3 %copy-start.5 = (bf16[256,2048]{1,0:T(8,128)(2,1)S(1)}, bf16[256,2048]{1,0:T(8,128)(2,1)}, u32[]{:S(2)}) copy-start(bf16[256,2048]{1,0:T(8,128)(2,1)} %param.11) | copy-start | bytes 3145732
  397.7 568.5 %copy-start.6 = (bf16[256,2048]{1,0:T(8,128)(2,1)S(1)}, bf16[256,2048]{1,0:T(8,128)(2,1)}, u32[]{:S(2)}) copy-start(bf16[256,2048]{1,0:T(8,128)(2,1)} %param.13) | copy-start | bytes 3145732
  683.5 361.3 %copy-start.1 = (f32[256,2048]{1,0:T(8,128)S(1)}, f32[256,2048]{1,0:T(8,128)}, u32[]{:S(2)}) copy-start(f32[256,2048]{1,0:T(8,128)} %reduce-scatter.3.cloned.1.call-done) | copy-start | bytes 6291460
Sparse Core Ops, SparseCore 0:
  10.2 127.6 all-gather.4
  139.9 123.1 all-gather.2
  324.4 30.9 all-reduce.8
  358.1 36.0 all-reduce.6
  398.4 282.3 reduce-scatter.2
  684.4 281.7 reduce-scatter.4
  969.2 32.2 all-reduce.10
where the time goes:
time: 1060 us
  waiting for transfers between devices  869 us (82%)
  blocking collectives  79 us (7%)
  matrix products  63.8 us (6%)
  other arithmetic  24.8 us (2%)
  between operations  17.2 us (2%)
    reduce_scatter x1, waiting for transfers between devices, on_device(): lax.psum_scatter(contract_rows(left_grad, right_grad), 'dp', scatter_dime...  283 us
    reduce_scatter x1, waiting for transfers between devices, on_device(): lax.psum_scatter(contract_rows(left_two_grad, right_two_grad), 'dp', scat...  283 us
    all_gather x1, waiting for transfers between devices, on_device(): full_in = lax.all_gather(w_in, 'dp', axis=0, tiled=True)  127 us
    all_gather x1, waiting for transfers between devices, on_device(): full_out = lax.all_gather(w_out, 'dp', axis=0, tiled=True)  120 us
    psum x1, blocking collectives, on_device(): lax.psum((jnp.sum(grad_one * w_in.astype(jnp.float32)), jnp.sum(grad_two...  39.6 us
    psum x1, waiting for transfers between devices, on_device(): lax.psum(dx_part.astype(jnp.bfloat16), 'rep').astype(jnp.float32)  32.5 us
    psum x1, blocking collectives, on_device(): branch_all, j_one_all = lax.psum((branch_part, j_one_part), 'rep')  26 us
    psum x1, waiting for transfers between devices, on_device(): j_two = lax.psum(j_two_part.astype(jnp.bfloat16), 'rep')  21.9 us
  transfers between devices with their start and end apart: 7, of which 6 were waited for; matrix products, arithmetic and copies ran while one was open for 5% of the time, Pallas kernels for 0%

commit v1 on v0

v1 whole, which is shorter than its diff:
```python
import jax
import jax.numpy as jnp
from jax import lax
from jax.sharding import Mesh
from jax.sharding import PartitionSpec as P

F32 = jnp.float32
BF16 = jnp.bfloat16
EVERY = ("z", "y", "x", "c")
SWAP = [(0, 1), (1, 0)]


def probe_signs(seeds, width):
    columns = jnp.arange(width, dtype=jnp.int32)
    mixed = seeds[:, None] * 747796405 + columns[None, :] * 1640531527
    mixed = mixed ^ lax.shift_right_logical(mixed, jnp.full_like(mixed, 16))
    mixed = mixed * 668265261
    mixed = mixed ^ lax.shift_right_logical(mixed, jnp.full_like(mixed, 15))
    lowbit = jnp.bitwise_and(lax.shift_right_logical(mixed, jnp.full_like(mixed, 7)), 1)
    return (1 - 2 * lowbit).astype(F32).astype(BF16)


def times(left, right):
    return jnp.dot(left, right, preferred_element_type=F32)


def contract_rows(left, right):
    return lax.dot_general(left, right, (((0,), (0,)), ((), ())), preferred_element_type=F32)


def contract_cols(left, right):
    return lax.dot_general(left, right, (((1,), (1,)), ((), ())), preferred_element_type=F32)


def in_order(own, other, index):
    first = jnp.where(index == 0, own, other)
    second = jnp.where(index == 0, other, own)
    return jnp.concatenate([first, second], 0)


def scatter_sum(part, planes, core):
    half = part.shape[0] // 2
    keep = lax.dynamic_slice_in_dim(part, core * half, half, 0)
    give = lax.dynamic_slice_in_dim(part, (1 - core) * half, half, 0).astype(BF16)
    pair = (keep + lax.ppermute(give, "c", SWAP).astype(F32)).astype(BF16)
    got = lax.all_to_all(pair, "z", 0, 0, tiled=True)
    return jnp.sum(got.reshape(planes, half // planes, -1).astype(F32), 0)


def gather_rows(quarter, core):
    half = lax.all_gather(quarter, "z", axis=0, tiled=True)
    return in_order(half, lax.ppermute(half, "c", SWAP), core)


def on_device(tokens, cotangent, probe_seed, w_in, bias, w_out, left_in, left_out):
    coef = 0.9
    planes = lax.axis_size("z")
    at_z, at_y, at_x, core = (lax.axis_index(name) for name in EVERY)
    count, width = tokens.shape
    rows_in, hid_rep = w_in.shape
    rows_out = w_out.shape[0]
    piece = hid_rep // planes
    quarter = count // 4
    at_dp = at_z * 2 + at_y
    at_rep = at_x * 2 + core

    full_out = lax.all_gather(w_out, ("x", "y"), axis=0, tiled=True)
    in_z = lax.all_to_all(w_in, "z", 1, 0, tiled=True)
    in_xy = lax.all_gather(in_z, ("x", "y"), axis=0)
    full_in = (
        in_xy.reshape(2, 2, planes, rows_in, piece)
        .transpose(2, 1, 3, 0, 4)
        .reshape(width, 2 * piece)
    )

    def own_quarter(array):
        return lax.dynamic_slice_in_dim(array, at_rep * quarter, quarter, 0)

    tok_own = own_quarter(tokens)
    pair = jnp.stack([tok_own, own_quarter(cotangent)])
    pair = lax.all_gather(pair, "z", axis=1)
    tok = in_order(pair[0], lax.ppermute(pair[0], "c", SWAP), core).reshape(-1, width)
    cot = in_order(pair[1], lax.ppermute(pair[1], "c", SWAP), core).reshape(-1, width)
    seeds = lax.all_gather(own_quarter(probe_seed), ("c", "z"), axis=0, tiled=True)
    probe = probe_signs(seeds, width)
    n = tok.shape[0]
    bias_all = lax.all_gather(
        lax.dynamic_slice_in_dim(bias, at_z * piece, piece, 0), "x", axis=0, tiled=True
    )

    left_one = left_in.astype(F32)
    slice_one = lax.dynamic_slice_in_dim(left_in, at_dp * rows_in, rows_in, 0)
    slice_two = lax.dynamic_slice_in_dim(left_out, at_dp * rows_out, rows_out, 0)
    p_part = times(slice_one, w_in)
    q_part = times(slice_two, w_out)
    slice_one = slice_one.astype(F32)
    slice_two = slice_two.astype(F32)
    reps = lax.axis_size("x") * 2
    p_slots = jnp.where(jnp.arange(reps)[:, None] == at_rep, p_part[None, :], 0.0)
    sums = lax.psum(
        jnp.concatenate([p_slots.reshape(-1), q_part, jnp.sum(slice_two * slice_two)[None]]), EVERY
    )
    p_all = sums[: reps * hid_rep].reshape(reps, hid_rep)
    q_vec = sums[reps * hid_rep : reps * hid_rep + width]
    p_norm = jnp.sum(p_all * p_all)
    q_norm = jnp.sum(q_vec * q_vec)
    p_vec = lax.dynamic_index_in_dim(p_all, at_rep, 0, keepdims=False)
    scale_in = coef * jnp.sqrt(jnp.sum(left_one * left_one) / p_norm)
    scale_out = coef * jnp.sqrt(sums[-1] / q_norm)

    raw = times(jnp.concatenate([tok, probe], 0), full_in)
    raw_z = raw[:n]
    e_one = scale_in * raw[n:]
    tanh_z = jnp.tanh(scale_in * raw_z + bias_all)
    deriv = 1.0 - tanh_z * tanh_z
    act = tanh_z.astype(BF16)
    r_one = (e_one * deriv).astype(BF16)
    j_part = scale_out * times(r_one, full_out)
    j_one = gather_rows(scatter_sum(j_part, planes, core).astype(BF16), core)
    branch = scatter_sum(scale_out * times(act, full_out), planes, core)
    output = lax.all_gather(
        (tok_own.astype(F32) + branch).astype(BF16), ("x", "c"), axis=0, tiled=True
    )
    backs = contract_cols(jnp.concatenate([probe, cot], 0), full_out)
    raw_b = backs[:n]
    raw_c = backs[n:]
    hd = deriv * (scale_out * raw_b)
    h_round = hd.astype(BF16)

    e_two = scale_in * times(j_one, full_in)
    r_two = (e_two * deriv).astype(BF16)
    j_part = scale_out * times(r_two, full_out)
    j_two = gather_rows(scatter_sum(j_part, planes, core).astype(BF16), core)
    e_three = scale_in * times(j_two, full_in)

    a_vec = e_one - e_two + e_three
    g_round = (a_vec * deriv).astype(BF16)
    second = -2.0 * tanh_z * deriv
    dz_vec = scale_out * raw_c * deriv - a_vec * (scale_out * raw_b) * second
    dz_round = dz_vec.astype(BF16)
    w_vec = (probe.astype(F32) - j_one.astype(F32) + j_two.astype(F32)).astype(BF16)

    terms = jnp.sum((e_one - e_two / 2.0 + e_three / 3.0) * hd, axis=1)
    inner_one = jnp.sum(dz_round.astype(F32) * raw_z - h_round.astype(F32) * (a_vec / scale_in))
    inner_two = jnp.sum(act.astype(F32) * raw_c - g_round.astype(F32) * raw_b)
    t_slots = jnp.where(
        jnp.arange(4)[:, None] == at_y * 2 + at_x, terms[None, :], 0.0
    ).reshape(-1)
    tail = lax.psum(jnp.concatenate([t_slots, inner_one[None], inner_two[None]]), EVERY)
    inner_one = tail[-2]
    inner_two = tail[-1]
    logdet = lax.dynamic_slice(
        tail[:-2].reshape(2, 2, 2, planes, quarter),
        (at_y, 0, 0, at_z, 0),
        (1, 2, 2, 1, quarter),
    ).reshape(count)

    grad_one = contract_rows(
        jnp.concatenate([tok, w_vec], 0), jnp.concatenate([dz_round, -h_round], 0)
    ).astype(BF16)
    grad_one = grad_one.reshape(planes, 2, rows_in, 2, piece).transpose(3, 1, 0, 2, 4)
    grad_one = lax.psum_scatter(
        grad_one.reshape(4 * planes * rows_in, piece), ("x", "y"), scatter_dimension=0, tiled=True
    )
    grad_one = lax.all_to_all(grad_one, "z", 0, 1, tiled=True).astype(F32)

    grad_two = contract_rows(
        jnp.concatenate([act, g_round], 0), jnp.concatenate([cot, -probe], 0)
    ).astype(BF16)
    grad_two = lax.psum_scatter(grad_two, ("x", "y"), scatter_dimension=0, tiled=True).astype(F32)

    dx = scatter_sum(scale_in * contract_cols(dz_round, full_in), planes, core)
    dx_all = lax.all_gather(dx.astype(BF16), ("x", "c"), axis=0, tiled=True)
    grad_tokens = cotangent.astype(F32) + dx_all.astype(F32)

    grad_in = scale_in * (grad_one - inner_one * slice_one[:, None] * p_vec[None, :] / p_norm)
    grad_out = scale_out * (grad_two - inner_two * slice_two[:, None] * q_vec[None, :] / q_norm)
    return (output, logdet, grad_tokens, grad_in, grad_out)


def solution(mesh):
    fine = Mesh(
        mesh.devices.reshape(mesh.shape["dp"] // 2, 2, mesh.shape["rep"] // 2, 2), EVERY
    )
    dp, rep = ("z", "y"), ("x", "c")
    placed = (
        P(dp, None),
        P(dp, None),
        P(dp),
        P(dp, rep),
        P(rep),
        P(rep + dp, None),
        P(),
        P(rep),
    )
    return jax.shard_map(
        on_device,
        mesh=fine,
        in_specs=placed,
        out_specs=(P(dp, None), P(dp), P(dp, None), P(dp, rep), P(rep + dp, None)),
        check_vma=False,
    )
```

time: 1060 us -> 417 us (0.39)
  waiting for transfers between devices: 869 us -> 109 us
  blocking collectives: 79 us -> 163 us
  local copies, waits for them, and re-layouts: 2.86 us -> 41.3 us
  matrix products: 63.8 us -> 33.3 us
  starting transfers between devices: 0.46 us -> 22.8 us
    reduce_scatter x2, waiting for transfers between devices: 566 us -> 6.09 us  [the longest x1 6.07 us: on_device(): lax.psum_scatter(grad_two, ('x', 'y'), scatter_dimension=0, tiled=True)]
    all_gather x2 -> x3, waiting for transfers between devices: 247 us -> 31 us  [the longest x1 31 us: on_device(): full_out = lax.all_gather(w_out, ('x', 'y'), axis=0, tiled=True)]
    all_to_all x0 -> x5, waiting for transfers between devices: none -> 65.7 us  [the longest x1 38.5 us: on_device(): in_z = lax.all_to_all(w_in, 'z', 1, 0, tiled=True)]
    all_gather x0 -> x5, blocking collectives: none -> 54.8 us  [the longest x2 31.7 us: gather_rows(): half = lax.all_gather(quarter, 'z', axis=0, tiled=True)]
    psum x3 -> x0, waiting for transfers between devices: 54.4 us -> none  [the longest x1 32.5 us: on_device(): lax.psum(dx_part.astype(jnp.bfloat16), 'rep').astype(jnp.float32)]
    all_to_all x0 -> x5, starting transfers between devices: none -> 21.1 us  [the longest x3 11.1 us: scatter_sum(): got = lax.all_to_all(pair, 'z', 0, 0, tiled=True)]
    reshape x0 -> x6, local copies, waits for them, and re-layouts: none -> 20.1 us  [the longest x2 12.9 us: on_device(): grad_one.reshape(planes, 2, rows_in, 2, piece).transpose(3, 1, 0, 2, 4)]
    all_to_all x0 -> x1, blocking collectives: none -> 19.2 us  [scatter_sum(): got = lax.all_to_all(pair, 'z', 0, 0, tiled=True)]
  transfers between devices with their start and end apart: 7 -> 18, of which waited for: 6 -> 8; matrix products, arithmetic and copies ran while one was open for 5% -> 13% of each run, Pallas kernels for 0% -> 0%
where the time goes in v1:
time: 417 us; the launch traced here: 415 us
  blocking collectives  163 us (39%)
  waiting for transfers between devices  109 us (26%)
  local copies, waits for them, and re-layouts  41.3 us (10%)
  matrix products  33.3 us (8%)
  other arithmetic  28.6 us (7%)
  starting transfers between devices  22.8 us (5%)
  between operations  17.6 us (4%)
    psum x1, blocking collectives, on_device(): lax.psum(jnp.concatenate([p_slots.reshape(-1), q_part, jnp.sum(slice_two...  41.6 us
    psum x1, blocking collectives, on_device(): lax.psum(jnp.concatenate([t_slots, inner_one[None], inner_two[None]]), EV...  40.4 us
    all_to_all x1, waiting for transfers between devices, on_device(): in_z = lax.all_to_all(w_in, 'z', 1, 0, tiled=True)  38.5 us
    all_gather x2, blocking collectives, gather_rows(): half = lax.all_gather(quarter, 'z', axis=0, tiled=True)  31.7 us
    all_gather x1, waiting for transfers between devices, on_device(): full_out = lax.all_gather(w_out, ('x', 'y'), axis=0, tiled=True)  31 us
    all_to_all x3, waiting for transfers between devices, scatter_sum(): got = lax.all_to_all(pair, 'z', 0, 0, tiled=True)  27.2 us
    all_to_all x1, blocking collectives, scatter_sum(): got = lax.all_to_all(pair, 'z', 0, 0, tiled=True)  19.2 us
    dot_general x8, matrix products, times(): return jnp.dot(left, right, preferred_element_type=F32)  18.1 us
  transfers between devices with their start and end apart: 18, of which 8 were waited for; matrix products, arithmetic and copies ran while one was open for 13% of the time, Pallas kernels for 0%

profile of v1, /device:TPU:0, one launch (start us, length us, event | category | flops | bytes accessed | tf_op | source)
XLA Modules:
  0.0 415.3 jit_solution(696043549375447723)
XLA Ops:
  9.4 6.3 %all-to-all-start = ((bf16[256,4,512]{0,2,1:T(8,128)(2,1)}), bf16[256,4,512]{0,2,1:T(8,128)(2,1)S(1)}, u32[]{:S(2)}, u32[]{:S(2)}) async-start(bf16[256,4,512]{0,2,1:T(8,128)(2,1)} %bitcast.9), calls=%async_computation | async-start | bytes 2097152 | tf_op jit(solution)/shard_map/all_to_all | solution.py:68
  17.5 38.5 %all-to-all-done = bf16[256,4,512]{0,2,1:T(8,128)(2,1)S(1)} async-done(((bf16[256,4,512]{0,2,1:T(8,128)(2,1)}), bf16[256,4,512]{0,2,1:T(8,128)(2,1)S(1)}, u32[]{:S(2)}, u32[]{:S(2)}) %all-to-all-start) | async-done | bytes 1048608 | tf_op jit(solution)/shard_map/all_to_all | solution.py:68
  61.4 7.0 %all-reduce = s32[256]{0:T(256)S(1)} all-reduce(s32[256]{0:T(256)S(1)} %dynamic-slice_dynamic-update-slice_fusion), channel_id=1, replica_groups=mesh['z'=4,'y'=2,'x'=2,'c'=2] {'c','z'}, use_global_device_ids=true, to_apply=%add | all-reduce | flops 256 | bytes 2048
  69.3 41.6 %psum.14 = f32[10241]{0:T(1024)S(1)} all-reduce(f32[10241]{0:T(1024)S(1)} %pad_maximum_fusion.11), channel_id=1, replica_groups=mesh['z'=4,'y'=2,'x'=2,'c'=2] {'z','y','x','c'}, use_global_device_ids=true, to_apply=%region_1.2 | all-reduce | flops 10241 | bytes 81928 | tf_op jit(solution)/shard_map/psum | solution.py:100
  118.9 4.7 %all-gather.1 = f32[2,1,512]{2,1,0:T(1,128)S(1)} all-gather(f32[1,1,512]{2,1,0:T(1,128)S(1)} %bitcast.89), channel_id=1, replica_groups=mesh['z'=4,'y'=2,'x'=2,'c'=2] {'x'}, dimensions={0}, use_global_device_ids=true | all-gather | bytes 6144 | tf_op jit(solution)/shard_map/all_gather | solution.py:87
  125.8 6.5 %copy.23 = bf16[2,2,4,256,512]{4,0,3,1,2:T(2,128)(2,1)S(1)} copy(bf16[2,2,4,256,512]{4,3,2,1,0:T(8,128)(2,1)} %bitcast.67) | data formatting | bytes 8388608 | tf_op jit(solution)/shard_map/reshape | solution.py:71
  135.5 2.3 fusion
  137.9 31.0 %all-gather.8.cloned.1.call-done = bf16[1024,2048]{1,0:T(8,128)(2,1)} async-done(((bf16[256,2048]{1,0:T(8,128)(2,1)}), bf16[1024,2048]{1,0:T(8,128)(2,1)}) %all-gather.8.cloned.1.call-update) | async-done | bytes 4194320 | tf_op jit(solution)/shard_map/all_gather | solution.py:67
  168.9 3.5 convolution_multiply_fusion.2
  177.1 19.2 %all_to_all.65 = bf16[4,32,2048]{2,1,0:T(8,128)(2,1)S(1)} all-to-all(bf16[4,32,2048]{2,1,0:T(8,128)(2,1)S(1)} %bitcast.71), channel_id=1, replica_groups=mesh['z'=4,'y'=2,'x'=2,'c'=2] {'z'}, dimensions={0} | all-to-all | bytes 1048576 | tf_op jit(solution)/shard_map/all_to_all | solution.py:46
  196.4 16.0 %all_gather.41 = bf16[128,2048]{1,0:T(8,128)(2,1)S(1)} all-gather(bf16[32,2048]{1,0:T(8,128)(2,1)S(1)} %reduce_sum.113), channel_id=1, replica_groups=mesh['z'=4,'y'=2,'x'=2,'c'=2] {'z'}, dimensions={0}, use_global_device_ids=true | all-gather | bytes 655360 | tf_op jit(solution)/shard_map/all_gather | solution.py:51
  215.3 3.6 convolution_multiply_fusion.5
  223.2 4.1 all-to-all-start.3
  229.8 12.7 %all-to-all-done.3 = bf16[4,32,2048]{2,1,0:T(8,128)(2,1)} async-done(((bf16[4,32,2048]{2,1,0:T(8,128)(2,1)}), bf16[4,32,2048]{2,1,0:T(8,128)(2,1)}, u32[]{:S(2)}, u32[]{:S(2)}) %all-to-all-start.3) | async-done | bytes 524320 | tf_op jit(solution)/shard_map/all_to_all | solution.py:46
  243.6 15.7 %all_gather.42 = bf16[128,2048]{1,0:T(8,128)(2,1)S(1)} all-gather(bf16[32,2048]{1,0:T(8,128)(2,1)S(1)} %reduce_sum.114), channel_id=1, replica_groups=mesh['z'=4,'y'=2,'x'=2,'c'=2] {'z'}, dimensions={0}, use_global_device_ids=true | all-gather | bytes 655360 | tf_op jit(solution)/shard_map/all_gather | solution.py:51
  259.4 5.2 %fusion.9 = f32[512,1024]{1,0:T(8,128)S(1)} fusion(bf16[1024,2048]{1,0:T(8,128)(2,1)} %all-gather.8.cloned.1.call-done, bf16[256,2048]{1,0:T(8,128)(2,1)} %bitcast.77, bf16[256,2048]{1,0:T(8,128)(2,1)} %copy-done.11), kind=kOutput, calls=%fused_computation.19 | convolution fusion | flops 2151677952 | bytes 8388608 | tf_op jit(solution)/shard_map/dot_general | solution.py:32
  266.7 3.3 subtract_reduce_fusion
  273.6 4.4 %convolution_convert_fusion.1 = bf16[2048,1024]{1,0:T(8,128)(2,1)} fusion(bf16[256,2048]{1,0:T(8,128)(2,1)S(1)} %bitcast.76, bf16[256,2048]{1,0:T(8,128)(2,1)S(1)} %add_convert_fusion, bf16[256,1024]{1,0:T(8,128)(2,1)S(1)} %get-tuple-element.7, bf16[256,1024]{1,0:T(8,128)(2,1)S(1)} %get-tuple-element.13), kind=kOutput, calls=%fused_computation.1 | convolution fusion | flops 2155872256 | bytes 7340032 | tf_op jit(solution)/shard_map/dot_general | solution.py:28
  278.0 7.9 %reshape.103 = bf16[4,2,256,2,512]{4,3,2,1,0:T(2,128)(2,1)} reshape(bf16[2048,1024]{1,0:T(8,128)(2,1)} %convolution_convert_fusion.1) | data formatting | bytes 8388608 | tf_op jit(solution)/shard_map/reshape | solution.py:161
  285.9 5.0 %copy.24 = bf16[4,2,256,2,512]{4,2,0,1,3:T(8,128)(2,1)} copy(bf16[4,2,256,2,512]{4,3,2,1,0:T(2,128)(2,1)} %reshape.103) | data formatting | bytes 8388608 | tf_op jit(solution)/shard_map/reshape | solution.py:161
  292.4 4.4 %convolution_convert_fusion = bf16[1024,2048]{1,0:T(8,128)(2,1)} fusion(bf16[256,2048]{1,0:T(8,128)(2,1)S(1)} %fusion.27, bf16[256,2048]{1,0:T(8,128)(2,1)S(1)} %bitcast.78, bf16[256,1024]{1,0:T(8,128)(2,1)S(1)} %copy-done.22, bf16[256,1024]{1,0:T(8,128)(2,1)S(1)} %copy-done.21), kind=kOutput, calls=%fused_computation | convolution fusion | flops 2155872256 | bytes 7340032 | tf_op jit(solution)/shard_map/dot_general | solution.py:28
  296.8 3.6 convolution_multiply_fusion.3
  304.2 3.5 all-to-all-start.1
  308.6 14.4 %all-to-all-done.1 = bf16[4,32,2048]{2,1,0:T(8,128)(2,1)S(1)} async-done(((bf16[4,32,2048]{2,1,0:T(8,128)(2,1)}), bf16[4,32,2048]{2,1,0:T(8,128)(2,1)S(1)}, u32[]{:S(2)}, u32[]{:S(2)}) %all-to-all-start.1) | async-done | bytes 524320 | tf_op jit(solution)/shard_map/all_to_all | solution.py:46
  323.0 3.5 all-to-all-start.4
  328.0 40.4 %psum.15 = f32[1026]{0:T(1024)S(1)} all-reduce(f32[1026]{0:T(1024)S(1)} %concatenate.43), channel_id=1, replica_groups=mesh['z'=4,'y'=2,'x'=2,'c'=2] {'z','y','x','c'}, use_global_device_ids=true, to_apply=%region_11.12 | all-reduce | flops 1026 | bytes 8208 | tf_op jit(solution)/shard_map/psum | solution.py:149
  371.2 3.7 all-to-all-start.5
  375.8 8.0 %all_gather.40 = bf16[128,2048]{1,0:T(8,128)(2,1)S(1)} all-gather(bf16[32,2048]{1,0:T(8,128)(2,1)S(1)} %add_convert_fusion.5), channel_id=1, replica_groups=mesh['z'=4,'y'=2,'x'=2,'c'=2] {'x','c'}, dimensions={0}, use_global_device_ids=true | all-gather | bytes 655360 | tf_op jit(solution)/shard_map/all_gather | solution.py:121
  383.9 10.4 %all_gather.43 = bf16[128,2048]{1,0:T(8,128)(2,1)S(1)} all-gather(bf16[32,2048]{1,0:T(8,128)(2,1)S(1)} %reduce_sum.118), channel_id=1, replica_groups=mesh['z'=4,'y'=2,'x'=2,'c'=2] {'x','c'}, dimensions={0}, use_global_device_ids=true | all-gather | bytes 655360 | tf_op jit(solution)/shard_map/all_gather | solution.py:173
  395.4 6.1 %reduce-scatter.5.cloned.1.call-done = bf16[256,2048]{1,0:T(8,128)(2,1)} async-done(((bf16[1024,2048]{1,0:T(8,128)(2,1)}), bf16[256,2048]{1,0:T(8,128)(2,1)}) %reduce-scatter.5.cloned.1.call-update) | async-done | bytes 1048592 | tf_op jit(solution)/shard_map/reduce_scatter | solution.py:170
  401.5 3.5 subtract_multiply_fusion
  405.6 2.4 subtract_multiply_fusion.1
  (146 shorter events, 55.3 us)
Async XLA Ops:
  9.4 46.6 %all-to-all-start = ((bf16[256,4,512]{0,2,1:T(8,128)(2,1)}), bf16[256,4,512]{0,2,1:T(8,128)(2,1)S(1)}, u32[]{:S(2)}, u32[]{:S(2)}) async-start(bf16[256,4,512]{0,2,1:T(8,128)(2,1)} %bitcast.9), calls=%async_computation | async-start | bytes 2097152 | tf_op jit(solution)/shard_map/all_to_all | solution.py:68
  15.7 97.0 %all-gather.10.cloned.1.call-start = ((), (), s32[]{:S(2)}) async-start(), calls=%async_computation.12 | async-start | bytes 1310720 | tf_op jit(solution)/shard_map/all_gather | solution.py:81
  17.5 108.3 %all-gather.6.cloned.1.call-start = ((), (), s32[]{:S(2)}) async-start(), calls=%async_computation.8 | async-start | bytes 5242880 | tf_op jit(solution)/shard_map/all_gather | solution.py:69
  56.1 3.5 copy-start.18
  56.1 3.6 copy-start.4
  57.4 2.6 copy-start.20
  57.4 3.8 copy-start.19
  57.4 11.0 %copy-start.5 = (bf16[256,2048]{1,0:T(8,128)(2,1)S(1)}, bf16[256,2048]{1,0:T(8,128)(2,1)}, u32[]{:S(2)}) copy-start(bf16[256,2048]{1,0:T(8,128)(2,1)} %param.13) | copy-start | bytes 3145732
  57.4 111.5 %all-gather.8.cloned.1.call-start = ((), (), s32[]{:S(2)}) async-start(), calls=%async_computation.9 | async-start | bytes 5242880 | tf_op jit(solution)/shard_map/all_gather | solution.py:67
  114.9 9.6 %collective-permute-start = (bf16[4,32,2048]{2,1,0:T(8,128)(2,1)S(1)}, bf16[4,32,2048]{2,1,0:T(8,128)(2,1)S(1)}, u32[]{:S(2)}, u32[]{:S(2)}) collective-permute-start(bf16[4,32,2048]{2,1,0:T(8,128)(2,1)S(1)} %bitcast.72), channel_id=1, source_target_pairs={{0,1},{1,0},{2,3},{3,2},{4,5},{5,4},{6,7},{7,6},{8,9},{9,8},{10,11... | collective-permute-start | bytes 1572872 | tf_op jit(solution)/shard_map/ppermute | solution.py:82
  124.4 9.1 %copy-start.11 = (bf16[256,2048]{1,0:T(8,128)(2,1)}, bf16[256,2048]{1,0:T(8,128)(2,1)S(1)}, u32[]{:S(2)}) copy-start(bf16[256,2048]{1,0:T(8,128)(2,1)S(1)} %fusion.7) | copy-start | bytes 3145732
  132.3 3.2 copy-start.12
  173.8 2.0 collective-permute-start.2
  212.3 1.9 collective-permute-start.3
  215.3 3.6 copy-start
  220.3 2.0 collective-permute-start.4
  220.5 6.9 %collective-permute-start.6 = (bf16[4,32,2048]{2,1,0:T(8,128)(2,1)}, bf16[4,32,2048]{2,1,0:T(8,128)(2,1)}, u32[]{:S(2)}, u32[]{:S(2)}) collective-permute-start(bf16[4,32,2048]{2,1,0:T(8,128)(2,1)} %bitcast.19), channel_id=1, source_target_pairs={{0,1},{1,0},{2,3},{3,2},{4,5},{5,4},{6,7},{7,6},{8,9},{9,8},{10,11... | collective-permute-start | bytes 1572872 | tf_op jit(solution)/shard_map/ppermute | solution.py:83
  223.2 19.3 %all-to-all-start.3 = ((bf16[4,32,2048]{2,1,0:T(8,128)(2,1)}), bf16[4,32,2048]{2,1,0:T(8,128)(2,1)}, u32[]{:S(2)}, u32[]{:S(2)}) async-start(bf16[4,32,2048]{2,1,0:T(8,128)(2,1)} %bitcast.70), calls=%async_computation.3 | async-start | bytes 1048576 | tf_op jit(solution)/shard_map/all_to_all | solution.py:46
  227.4 143.8 %reduce-scatter.3.cloned.1.call-start = ((), (), s32[]{:S(2)}) async-start(), calls=%async_computation.10 | async-start | bytes 5242880 | tf_op jit(solution)/shard_map/reduce_scatter | solution.py:162
  259.3 5.5 %collective-permute-start.5 = (bf16[128,2048]{1,0:T(8,128)(2,1)S(1)}, bf16[128,2048]{1,0:T(8,128)(2,1)S(1)}, u32[]{:S(2)}, u32[]{:S(2)}) collective-permute-start(bf16[128,2048]{1,0:T(8,128)(2,1)S(1)} %all_gather.42), channel_id=1, source_target_pairs={{0,1},{1,0},{2,3},{3,2},{4,5},{5,4},{6,7},{7,6},{8,9},{9,8},{10,11... | collective-permute-start | bytes 1572872 | tf_op jit(solution)/shard_map/ppermute | solution.py:52
  266.7 3.3 copy-start.7
  266.7 3.3 copy-start.9
  271.1 2.5 copy-start.13
  290.9 110.6 %reduce-scatter.5.cloned.1.call-start = ((), (), s32[]{:S(2)}) async-start(), calls=%async_computation.11 | async-start | bytes 5242880 | tf_op jit(solution)/shard_map/reduce_scatter | solution.py:170
  296.8 4.3 %copy-start.3 = (bf16[256,8,2,512]{3,1,2,0:T(8,128)(2,1)S(1)}, bf16[256,8,2,512]{3,1,2,0:T(8,128)(2,1)}, u32[]{:S(2)}) copy-start(bf16[256,8,2,512]{3,1,2,0:T(8,128)(2,1)} %copy-done.1) | copy-start | bytes 12582916
  296.8 4.2 %copy-start.17 = (bf16[256,1024]{1,0:T(8,128)(2,1)S(1)}, bf16[256,1024]{1,0:T(8,128)(2,1)}, u32[]{:S(2)}) copy-start(bf16[256,1024]{1,0:T(8,128)(2,1)} %copy-done.16) | copy-start | bytes 1572868
  300.5 2.8 collective-permute-start.1
  303.2 4.5 %collective-permute-start.7 = (bf16[128,2048]{1,0:T(8,128)(2,1)}, bf16[128,2048]{1,0:T(8,128)(2,1)S(1)}, u32[]{:S(2)}, u32[]{:S(2)}) collective-permute-start(bf16[128,2048]{1,0:T(8,128)(2,1)} %dynamic-slice_convert_fusion), channel_id=1, source_target_pairs={{0,1},{1,0},{2,3},{3,2},{4,5},{5,4},{6,7},{7,6},{8,9},{9,8},{10,11... | collective-permute-start | bytes 1572872 | tf_op jit(solution)/shard_map/ppermute | solution.py:45
  304.2 18.9 %all-to-all-start.1 = ((bf16[4,32,2048]{2,1,0:T(8,128)(2,1)}), bf16[4,32,2048]{2,1,0:T(8,128)(2,1)S(1)}, u32[]{:S(2)}, u32[]{:S(2)}) async-start(bf16[4,32,2048]{2,1,0:T(8,128)(2,1)} %bitcast.16), calls=%async_computation.1 | async-start | bytes 1048576 | tf_op jit(solution)/shard_map/all_to_all | solution.py:46
  323.0 48.1 %all-to-all-start.4 = ((bf16[4,32,2048]{2,1,0:T(8,128)(2,1)}), bf16[4,32,2048]{2,1,0:T(8,128)(2,1)S(1)}, u32[]{:S(2)}, u32[]{:S(2)}) async-start(bf16[4,32,2048]{2,1,0:T(8,128)(2,1)} %bitcast.23), calls=%async_computation.4 | async-start | bytes 1048576 | tf_op jit(solution)/shard_map/all_to_all | solution.py:46
  371.2 23.2 %copy-start.15 = (bf16[128,2048]{1,0:T(8,128)(2,1)S(1)}, bf16[128,2048]{1,0:T(8,128)(2,1)}, u32[]{:S(2)}) copy-start(bf16[128,2048]{1,0:T(8,128)(2,1)} %param.9) | copy-start | bytes 1572868
  371.2 33.9 %all-to-all-start.5 = ((bf16[4,256,512]{2,1,0:T(8,128)(2,1)}), bf16[4,256,512]{2,1,0:T(8,128)(2,1)S(1)}, u32[]{:S(2)}, u32[]{:S(2)}) async-start(bf16[4,256,512]{2,1,0:T(8,128)(2,1)} %bitcast.74), calls=%async_computation.6 | async-start | bytes 2097152 | tf_op jit(solution)/shard_map/all_to_all | solution.py:165
  (9 other events, 12.2 us)
Sparse Core Ops, SparseCore 0:
  18.7 39.9 all-gather.9
  61.1 53.1 all-gather.5
  116.1 52.6 all-gather.7
  291.0 51.1 reduce-scatter.2
  345.3 56.1 reduce-scatter.4
